TPU v7x, 128 devices: a whole 4x4x4 slice. The times are simulated.
128 devices in a mesh: rows: 32 (over x, y, core), rep: 4 (over z).
Axes of the slice: x: 4, y: 4, z: 4, core: 2. Of those that a mesh axis runs over, the one named last changes fastest.
Arguments:
- vectors: bfloat16 [65536, 1024], P(('rows', 'rep')), may hold values from -96 to 96
- list_ids: int32 [65536], P(('rows', 'rep')), may hold values from 0 to 262143, as said below
- centroids: bfloat16 [262144, 1024], P(('rows', 'rep')), may hold values from -16 to 16
- list_place: int32 [262144], replicated, may hold values from 0 to 262143, as said below
- codes_first: int32 [65536, 128], P(('rows', 'rep')), may hold values from 0 to 255
- codes_second: int32 [65536, 128], P(('rows', 'rep')), may hold values from 0 to 255
Outputs:
- codebook_first: float32 [256, 1024], P(None, 'rows')
- codebook_second: float32 [256, 1024], P(None, 'rows')
Inputs may be any that keep to these rules, and one draw needn't show every extreme that they name: list_place is a permutation of the table rows. Among the rows of one device, at most 8 have list_place[list_ids] inside one device's block of 2048 table rows, and exactly 8 for some blocks of every device.
All inputs are finite; a program needn't handle non-finite values.
Results may differ from a plain program's by a relative error of at most 0.0003.
Values may be sent and summed in bfloat16 or wider, within the bound.
A program may use at most 64 MiB of HBM per device.

v0:
```python
import math
import jax
import jax.numpy as jnp
from jax import lax
from jax.sharding import PartitionSpec as P

SUB = 8
K = 256


def code_sums(residual, code_pair):
    total_rows = residual.shape[0]
    subspaces = code_pair[0].shape[1]
    block_rows = math.gcd(total_rows, 32768 // subspaces)
    turn_count = total_rows // block_rows
    shaped = residual.reshape(turn_count, block_rows, subspaces, SUB)
    codewords = jnp.arange(K, dtype=jnp.int32)
    zeros_sums = jnp.zeros((subspaces, K, SUB), jnp.float32)
    zeros_counts = jnp.zeros((subspaces, K), jnp.float32)

    def add_block(running, block_index):
        row_block = lax.dynamic_index_in_dim(shaped, block_index, 0, keepdims=False)
        updated = []
        for code_all, state in zip(code_pair, running):
            code_block = lax.dynamic_slice_in_dim(code_all, block_index * block_rows, block_rows, 0)
            one_hot = (code_block[:, :, None] == codewords).astype(row_block.dtype)
            block_sums = jnp.einsum(
                "rsk,rsc->skc",
                one_hot,
                row_block,
                preferred_element_type=jnp.float32,
                precision=lax.Precision.HIGHEST,
            )
            block_counts = jnp.sum(one_hot, axis=0, dtype=jnp.float32)
            updated.append((state[0] + block_sums, state[1] + block_counts))
        return (tuple(updated), None)

    start_state = ((zeros_sums, zeros_counts), (zeros_sums, zeros_counts))
    final_state, unused = lax.scan(add_block, start_state, jnp.arange(turn_count, dtype=jnp.int32))
    laid_out = []
    for sums_part, counts_part in final_state:
        laid_out.append(jnp.transpose(sums_part, (1, 0, 2)).reshape(K, subspaces * SUB))
        laid_out.append(counts_part.T)
    return tuple(laid_out)


def finish(first_sums, first_counts, second_sums, second_counts):
    totals = lax.psum((first_sums, first_counts, second_sums, second_counts), "rep")
    codebooks = []
    for sums_part, counts_part in ((totals[0], totals[1]), (totals[2], totals[3])):
        spread = jnp.repeat(jnp.maximum(counts_part, 1.0), SUB, axis=1)
        codebooks.append(sums_part / spread)
    return (codebooks[0], codebooks[1])


def plan_slots(list_ids, list_place, shard_rows, devices, capacity):
    local_rows = list_ids.shape[0]
    places = jnp.take(list_place, list_ids, axis=0)
    owner_ids = places // shard_rows
    slot_in = places - owner_ids * shard_rows
    by_owner = jnp.argsort(owner_ids, stable=True)
    sorted_owner = owner_ids[by_owner]
    per_owner = jnp.sum(
        (owner_ids[:, None] == jnp.arange(devices, dtype=jnp.int32)[None, :]).astype(jnp.int32),
        axis=0,
    )
    first_row = jnp.cumsum(per_owner) - per_owner
    rank_sorted = jnp.arange(local_rows, dtype=jnp.int32) - first_row[sorted_owner]
    position = (
        jnp.zeros((local_rows,), jnp.int32).at[by_owner].set(sorted_owner * capacity + rank_sorted)
    )
    request = (
        jnp.zeros((devices * capacity,), jnp.int32)
        .at[position]
        .set(slot_in)
        .reshape(devices, capacity)
    )
    return (position, request)


def fetch_residual(vectors, centroids, position, request, devices, capacity):
    wanted_ids = lax.all_to_all(request, ("rows", "rep"), split_axis=0, concat_axis=0, tiled=True)
    answer = jnp.take(centroids, wanted_ids.reshape(-1), axis=0)
    answer = answer.reshape(wanted_ids.shape[0], wanted_ids.shape[1], centroids.shape[1])
    fetched = lax.all_to_all(answer, ("rows", "rep"), split_axis=0, concat_axis=0, tiled=True)
    fetched_rows = jnp.take(
        fetched.reshape(devices * capacity, centroids.shape[1]), position, axis=0
    )
    return vectors.astype(jnp.float32) - fetched_rows.astype(jnp.float32)


def on_device(vectors, list_ids, centroids, list_place, codes_first, codes_second):
    devices = lax.axis_size(("rows", "rep"))
    local_rows = vectors.shape[0]
    shard_rows = centroids.shape[0]
    capacity = 2 * local_rows // devices
    position, request = plan_slots(list_ids, list_place, shard_rows, devices, capacity)
    residual = fetch_residual(vectors, centroids, position, request, devices, capacity)
    transposed = (
        lax.all_to_all(residual, "rows", split_axis=1, concat_axis=0, tiled=True),
        lax.all_to_all(codes_first, "rows", split_axis=1, concat_axis=0, tiled=True),
        lax.all_to_all(codes_second, "rows", split_axis=1, concat_axis=0, tiled=True),
    )
    local_parts = code_sums(transposed[0], (transposed[1], transposed[2]))
    return finish(local_parts[0], local_parts[1], local_parts[2], local_parts[3])


def solution(mesh):
    return jax.shard_map(
        on_device,
        mesh=mesh,
        in_specs=(
            P(("rows", "rep"), None),
            P(("rows", "rep")),
            P(("rows", "rep"), None),
            P(),
            P(("rows", "rep"), None),
            P(("rows", "rep"), None),
        ),
        out_specs=(P(None, "rows"), P(None, "rows")),
        check_vma=False,
    )
```

profile of v0, /device:TPU:0, one launch (start us, length us, event | category | flops | bytes accessed | tf_op | source)
XLA Modules:
  0.0 313.5 jit_solution(9564695646376202633)
XLA Ops:
  8.4 3.1 gather_fusion
  12.2 3.8 %sort.17 = (s32[512]{0:T(512)}, s32[512]{0:T(512)S(1)}) sort(s32[512]{0:T(512)S(1)} %get-tuple-element.172, s32[512]{0:T(512)S(1)} %iota.21), dimensions={0}, to_apply=%region_0.1 | sort | flops 4608 | bytes 8192 | tf_op jit(solution)/shard_map/jit(argsort)/sort | solution.py:61
  15.9 3.5 %gather_fusion.1 = s32[512]{0:T(512)S(1)} fusion(s32[512]{0:T(512)S(1)} %get-tuple-element.172, s32[1024]{0:T(1024)S(1)} %pad_clamp_fusion.2), kind=kCustom, calls=%fused_computation.1 | custom fusion | bytes 6144 | tf_op jit(solution)/shard_map/gather | solution.py:62
  19.5 3.3 %gather_fusion.2 = s32[512]{0:T(512)S(1)} fusion(s32[128]{0:T(128)S(1)} %sub.19, s32[1024]{0:T(1024)S(1)} %pad_clamp_fusion.1), kind=kCustom, calls=%fused_computation.2 | custom fusion | bytes 6144 | tf_op jit(solution)/shard_map/gather | solution.py:68
  27.8 20.0 %all_to_all.68 = s32[128,1,8]{2,1,0:T(1,128)S(1)} all-to-all(s32[128,1,8]{2,1,0:T(1,128)S(1)} %bitcast.51), channel_id=1, replica_groups=mesh['rows'=32,'rep'=4] {'rows','rep'}, dimensions={0} | all-to-all | bytes 8192 | tf_op jit(solution)/shard_map/all_to_all | solution.py:82
  49.3 7.7 %gather_fusion.3 = bf16[1024,1024]{1,0:T(8,128)(2,1)S(1)} fusion(bf16[2048,1024]{1,0:T(8,128)(2,1)} %param.10, s32[1024]{0:T(1024)S(1)} %broadcast_clamp_fusion), kind=kCustom, calls=%fused_computation.3 | custom fusion | bytes 4198400 | tf_op jit(solution)/shard_map/jit(_take)/gather | solution.py:83
  58.7 4.9 %all-to-all-start.2 = ((bf16[128,8,1024]{2,1,0:T(8,128)(2,1)}), bf16[128,8,1024]{2,1,0:T(8,128)(2,1)S(1)}, u32[]{:S(2)}, u32[]{:S(2)}) async-start(bf16[128,8,1024]{2,1,0:T(8,128)(2,1)} %bitcast_select_fusion), calls=%async_computation.2 | async-start | bytes 4194304 | tf_op jit(solution)/shard_map/all_to_all | solution.py:85
  65.5 28.3 %all-to-all-done.2 = bf16[128,8,1024]{2,1,0:T(8,128)(2,1)S(1)} async-done(((bf16[128,8,1024]{2,1,0:T(8,128)(2,1)}), bf16[128,8,1024]{2,1,0:T(8,128)(2,1)S(1)}, u32[]{:S(2)}, u32[]{:S(2)}) %all-to-all-start.2) | async-done | bytes 2097184 | tf_op jit(solution)/shard_map/all_to_all | solution.py:85
  93.7 3.9 %all-to-all-start = ((s32[512,32,4]{0,2,1:T(4,128)}), s32[512,32,4]{0,2,1:T(4,128)S(1)}, u32[]{:S(2)}, u32[]{:S(2)}) async-start(s32[512,32,4]{0,2,1:T(4,128)} %all_to_all.49), calls=%async_computation | async-start | bytes 524288 | tf_op jit(solution)/shard_map/all_to_all | solution.py:101
  97.6 2.8 gather_fusion.4
  106.5 5.0 %all-to-all-start.3 = ((f32[512,32,32]{0,2,1:T(8,128)}), f32[512,32,32]{0,2,1:T(8,128)S(1)}, u32[]{:S(2)}, u32[]{:S(2)}) async-start(f32[512,32,32]{0,2,1:T(8,128)} %bitcast.48), calls=%async_computation.3 | async-start | bytes 4194304 | tf_op jit(solution)/shard_map/all_to_all | solution.py:100
  115.1 25.4 %all-to-all-done.3 = f32[512,32,32]{0,2,1:T(8,128)S(1)} async-done(((f32[512,32,32]{0,2,1:T(8,128)}), f32[512,32,32]{0,2,1:T(8,128)S(1)}, u32[]{:S(2)}, u32[]{:S(2)}) %all-to-all-start.3) | async-done | bytes 2097184 | tf_op jit(solution)/shard_map/all_to_all | solution.py:100
  140.5 4.6 %all-to-all-start.4 = ((s32[512,32,4]{0,2,1:T(4,128)}), s32[512,32,4]{0,2,1:T(4,128)}, u32[]{:S(2)}, u32[]{:S(2)}) async-start(s32[512,32,4]{0,2,1:T(4,128)} %all_to_all.59), calls=%async_computation.4 | async-start | bytes 524288 | tf_op jit(solution)/shard_map/all_to_all | solution.py:102
  147.8 4.0 %reshape.159 = f32[2,8192,4,8]{1,0,3,2:T(2,128)} reshape(f32[32,512,32]{1,0,2:T(8,128)} %copy.28) | data formatting | bytes 4194304 | tf_op jit(solution)/shard_map/reshape | solution.py:16
  154.0 111.4 %while.18 = (s32[]{:T(128)}, f32[4,256,8]{1,2,0:T(8,128)S(1)}, f32[4,256]{1,0:T(4,128)S(1)}, f32[4,256,8]{1,2,0:T(8,128)S(1)}, f32[4,256]{1,0:T(4,128)S(1)}, /*i...) while((s32[]{:T(128)}, f32[4,256,8]{1,2,0:T(8,128)S(1)}, ...), condition=%wide.region_8.9_spmd.clone.clone, body=%wide.region_5.8_spmd.clone.clone.sunk | while | flops 1677756416 | bytes 5406969 | solution.py:39
  160.8 10.9 %fusion.25 = f32[4,256,8]{1,2,0:T(8,128)S(1)} fusion(s32[8192,4]{0,1:T(4,128)S(1)} %constant_dynamic-slice_fusion.8, f32[1,8192,4,8]{1,0,3,2:T(1,128)S(1)} %constant_dynamic-slice_fusion.7, f32[4,256,8]{1,2,0:T(8,128)S(1)} %get-tuple-element.253, pred[]{:T(512)S(6)} %compare.12), kind=kOutput, calls=%fused_computation.18.clone.1 | convolution fusion | flops 813711360 | bytes 1245185 | tf_op jit(solution)/shard_map/while/body/eval_jaxpr/rsk,rsc->skc/dot_general | solution.py:27
  171.7 10.9 %fusion.22 = f32[4,256,8]{1,2,0:T(8,128)S(1)} fusion(s32[8192,4]{0,1:T(4,128)S(1)} %constant_dynamic-slice_fusion.6, f32[1,8192,4,8]{1,0,3,2:T(1,128)S(1)} %constant_dynamic-slice_fusion.7, f32[4,256,8]{1,2,0:T(8,128)S(1)} %get-tuple-element.251, pred[]{:T(512)S(6)} %compare.12), kind=kOutput, calls=%fused_computation.19.clone.1 | convolution fusion | flops 813711360 | bytes 1245185 | tf_op jit(solution)/shard_map/while/body/eval_jaxpr/rsk,rsc->skc/dot_general | solution.py:27
  182.5 13.5 %fusion.23 = f32[4,256]{1,0:T(4,128)S(1)} fusion(s32[8192,4]{0,1:T(4,128)S(1)} %constant_dynamic-slice_fusion.8), kind=kLoop, calls=%fused_computation.14.clone.1 | loop fusion | flops 25164800 | bytes 135168 | tf_op jit(solution)/shard_map/while/body/eval_jaxpr/reduce_sum | solution.py:34
  196.1 13.6 %fusion.24 = f32[4,256]{1,0:T(4,128)S(1)} fusion(s32[8192,4]{0,1:T(4,128)S(1)} %constant_dynamic-slice_fusion.6), kind=kLoop, calls=%fused_computation.15.clone.1 | loop fusion | flops 25164800 | bytes 135168 | tf_op jit(solution)/shard_map/while/body/eval_jaxpr/reduce_sum | solution.py:34
  216.5 10.9 %fusion.25 = f32[4,256,8]{1,2,0:T(8,128)S(1)} fusion(s32[8192,4]{0,1:T(4,128)S(1)} %constant_dynamic-slice_fusion.8, f32[1,8192,4,8]{1,0,3,2:T(1,128)S(1)} %constant_dynamic-slice_fusion.7, f32[4,256,8]{1,2,0:T(8,128)S(1)} %get-tuple-element.253, pred[]{:T(512)S(6)} %compare.12), kind=kOutput, calls=%fused_computation.18.clone.1 | convolution fusion | flops 813711360 | bytes 1245185 | tf_op jit(solution)/shard_map/while/body/eval_jaxpr/rsk,rsc->skc/dot_general | solution.py:27
  227.4 10.9 %fusion.22 = f32[4,256,8]{1,2,0:T(8,128)S(1)} fusion(s32[8192,4]{0,1:T(4,128)S(1)} %constant_dynamic-slice_fusion.6, f32[1,8192,4,8]{1,0,3,2:T(1,128)S(1)} %constant_dynamic-slice_fusion.7, f32[4,256,8]{1,2,0:T(8,128)S(1)} %get-tuple-element.251, pred[]{:T(512)S(6)} %compare.12), kind=kOutput, calls=%fused_computation.19.clone.1 | convolution fusion | flops 813711360 | bytes 1245185 | tf_op jit(solution)/shard_map/while/body/eval_jaxpr/rsk,rsc->skc/dot_general | solution.py:27
  238.3 13.5 %fusion.23 = f32[4,256]{1,0:T(4,128)S(1)} fusion(s32[8192,4]{0,1:T(4,128)S(1)} %constant_dynamic-slice_fusion.8), kind=kLoop, calls=%fused_computation.14.clone.1 | loop fusion | flops 25164800 | bytes 135168 | tf_op jit(solution)/shard_map/while/body/eval_jaxpr/reduce_sum | solution.py:34
  251.8 13.6 %fusion.24 = f32[4,256]{1,0:T(4,128)S(1)} fusion(s32[8192,4]{0,1:T(4,128)S(1)} %constant_dynamic-slice_fusion.6), kind=kLoop, calls=%fused_computation.15.clone.1 | loop fusion | flops 25164800 | bytes 135168 | tf_op jit(solution)/shard_map/while/body/eval_jaxpr/reduce_sum | solution.py:34
  266.1 37.8 %all-reduce.3.cloned.1.call-done = (f32[256,32]{0,1:T(8,128)}, f32[256,4]{0,1:T(4,128)}, f32[256,32]{0,1:T(8,128)}, f32[256,4]{0,1:T(4,128)}) async-done(((f32[256,32]{0,1:T(8,128)}, f32[256,4]{0,1:T(4,128)}, f32[256,32]{0,1:T(8,128)}, f32[256,4]{0,1:T(4,128)}), (f32[256,32]{0,1:T(8,128)}, f32[256,4]{0,1:T(4,128)}, f32[256,32]{0,1:T(8,128)}, f32[256,4]{0,1:T(4,128)})) %all-reduce.3.cloned.1.call-update) | async-done | bytes 73744 | tf_op jit(solution)/shard_map/psum | solution.py:48
  (68 shorter events, 38.1 us)
Async XLA Ops:
  7.2 1.2 copy-start
  7.2 4.4 %copy-start.5 = (s32[512]{0:T(512)S(1)}, s32[512]{0:T(512)}, u32[]{:S(2)}) copy-start(s32[512]{0:T(512)} %param.9) | copy-start | bytes 6148
  58.7 35.1 %all-to-all-start.2 = ((bf16[128,8,1024]{2,1,0:T(8,128)(2,1)}), bf16[128,8,1024]{2,1,0:T(8,128)(2,1)S(1)}, u32[]{:S(2)}, u32[]{:S(2)}) async-start(bf16[128,8,1024]{2,1,0:T(8,128)(2,1)} %bitcast_select_fusion), calls=%async_computation.2 | async-start | bytes 4194304 | tf_op jit(solution)/shard_map/all_to_all | solution.py:85
  93.7 12.8 %all-to-all-start = ((s32[512,32,4]{0,2,1:T(4,128)}), s32[512,32,4]{0,2,1:T(4,128)S(1)}, u32[]{:S(2)}, u32[]{:S(2)}) async-start(s32[512,32,4]{0,2,1:T(4,128)} %all_to_all.49), calls=%async_computation | async-start | bytes 524288 | tf_op jit(solution)/shard_map/all_to_all | solution.py:101
  106.5 33.9 %all-to-all-start.3 = ((f32[512,32,32]{0,2,1:T(8,128)}), f32[512,32,32]{0,2,1:T(8,128)S(1)}, u32[]{:S(2)}, u32[]{:S(2)}) async-start(f32[512,32,32]{0,2,1:T(8,128)} %bitcast.48), calls=%async_computation.3 | async-start | bytes 4194304 | tf_op jit(solution)/shard_map/all_to_all | solution.py:100
  140.5 13.5 %all-to-all-start.4 = ((s32[512,32,4]{0,2,1:T(4,128)}), s32[512,32,4]{0,2,1:T(4,128)}, u32[]{:S(2)}, u32[]{:S(2)}) async-start(s32[512,32,4]{0,2,1:T(4,128)} %all_to_all.59), calls=%async_computation.4 | async-start | bytes 524288 | tf_op jit(solution)/shard_map/all_to_all | solution.py:102
  145.1 158.8 %all-reduce.3.cloned.1.call-start = ((), (), s32[]{:S(2)}) async-start(), calls=%async_computation.5 | async-start | bytes 147456 | tf_op jit(solution)/shard_map/psum | solution.py:48
  265.4 0.6 copy-start.1
  265.4 0.6 copy-start.2
  265.4 0.6 copy-start.3
  265.5 0.6 copy-start.4
Sparse Core Ops, SparseCore 0:
  266.2 37.6 all-reduce.2
where the time goes:
time: 314 us
  waiting for transfers between devices  95.9 us (31%)
  other arithmetic  66.5 us (21%)
  local copies, waits for them, and re-layouts  49.5 us (16%)
  matrix products  43.4 us (14%)
  blocking collectives  20 us (6%)
  starting transfers between devices  18.6 us (6%)
  between operations  14.3 us (5%)
  loops' own time  5.27 us (2%)
    reduce_sum x4, other arithmetic, add_block(): block_counts = jnp.sum(one_hot, axis=0, dtype=jnp.float32)  54.3 us
    dot_general x4, matrix products, add_block(): jnp.einsum('rsk,rsc->skc', one_hot, row_block, preferred_element_type=jnp...  43.4 us
    psum x1, waiting for transfers between devices, finish(): lax.psum((first_sums, first_counts, second_sums, second_counts), 'rep')  37.8 us
    all_to_all x1, waiting for transfers between devices, fetch_residual(): lax.all_to_all(answer, ('rows', 'rep'), split_axis=0, concat_axis=0, tile...  28.3 us
    all_to_all x1, waiting for transfers between devices, on_device(): lax.all_to_all(residual, 'rows', split_axis=1, concat_axis=0, tiled=True)  25.4 us
    all_to_all x1, blocking collectives, fetch_residual(): lax.all_to_all(request, ('rows', 'rep'), split_axis=0, concat_axis=0, til...  20 us
    gather x1, local copies, waits for them, and re-layouts, fetch_residual(): answer = jnp.take(centroids, wanted_ids.reshape(-1), axis=0)  7.71 us
  transfers between devices with their start and end apart: 5, of which 5 were waited for; matrix products, arithmetic and copies ran while one was open for 5% of the time, Pallas kernels for 0%

commit v1 on v0

--- a/solution.py
+++ b/solution.py
@@ -98,7 +98,12 @@
     residual = fetch_residual(vectors, centroids, position, request, devices, capacity)
     transposed = (
         lax.all_to_all(residual, "rows", split_axis=1, concat_axis=0, tiled=True),
-        lax.all_to_all(codes_first, "rows", split_axis=1, concat_axis=0, tiled=True),
+        jnp.concatenate(
+            lax.all_to_all(
+                jnp.stack(jnp.split(codes_first, lax.axis_size("rows"), axis=1)), "rows", 0, 0
+            ),
+            axis=0,
+        ),
         lax.all_to_all(codes_second, "rows", split_axis=1, concat_axis=0, tiled=True),
     )
     local_parts = code_sums(transposed[0], (transposed[1], transposed[2]))

time: 314 us -> 343 us (1.092)
  local copies, waits for them, and re-layouts: 49.5 us -> 99 us
  waiting for transfers between devices: 95.9 us -> 69.9 us
    another operation x1 -> x37, local copies, waits for them, and re-layouts: 0.12 us -> 51.5 us  [the longest x36 51.3 us: on_device(): jnp.stack(jnp.split(codes_first, lax.axis_size('rows'), axis=1))]
    all_to_all x1, waiting for transfers between devices: 28.3 us -> 0.01 us  [fetch_residual(): lax.all_to_all(answer, ('rows', 'rep'), split_axis=0, concat_axis=0, tile...]
  transfers between devices with their start and end apart: 5 -> 5, of which waited for: 5 -> 4; matrix products, arithmetic and copies ran while one was open for 5% -> 20% of each run, Pallas kernels for 0% -> 0%
where the time goes in v1:
time: 343 us; the launch traced here: 341 us
  local copies, waits for them, and re-layouts  99 us (29%)
  waiting for transfers between devices  69.9 us (20%)
  other arithmetic  67.8 us (20%)
  matrix products  43.4 us (13%)
  starting transfers between devices  21.3 us (6%)
  blocking collectives  20 us (6%)
  between operations  14.4 us (4%)
  loops' own time  5.27 us (2%)
    reduce_sum x4, other arithmetic, add_block(): block_counts = jnp.sum(one_hot, axis=0, dtype=jnp.float32)  54.3 us
    another operation x36, local copies, waits for them, and re-layouts, on_device(): jnp.stack(jnp.split(codes_first, lax.axis_size('rows'), axis=1))  51.3 us
    dot_general x4, matrix products, add_block(): jnp.einsum('rsk,rsc->skc', one_hot, row_block, preferred_element_type=jnp...  43.4 us
    psum x1, waiting for transfers between devices, finish(): lax.psum((first_sums, first_counts, second_sums, second_counts), 'rep')  40 us
    all_to_all x1, waiting for transfers between devices, on_device(): lax.all_to_all(residual, 'rows', split_axis=1, concat_axis=0, tiled=True)  25.4 us
    all_to_all x1, blocking collectives, fetch_residual(): lax.all_to_all(request, ('rows', 'rep'), split_axis=0, concat_axis=0, til...  20 us
    gather x1, local copies, waits for them, and re-layouts, fetch_residual(): answer = jnp.take(centroids, wanted_ids.reshape(-1), axis=0)  7.71 us
  transfers between devices with their start and end apart: 5, of which 4 were waited for; matrix products, arithmetic and copies ran while one was open for 20% of the time, Pallas kernels for 0%

profile of v1, /device:TPU:0, one launch (start us, length us, event | category | flops | bytes accessed | tf_op | source)
XLA Modules:
  0.0 341.0 jit_solution(1596736396713728341)
XLA Ops:
  8.4 3.1 gather_fusion
  12.2 3.8 %sort.17 = (s32[512]{0:T(512)}, s32[512]{0:T(512)S(1)}) sort(s32[512]{0:T(512)S(1)} %get-tuple-element.172, s32[512]{0:T(512)S(1)} %iota.21), dimensions={0}, to_apply=%region_0.1 | sort | flops 4608 | bytes 8192 | tf_op jit(solution)/shard_map/jit(argsort)/sort | solution.py:61
  15.9 3.5 %gather_fusion.1 = s32[512]{0:T(512)S(1)} fusion(s32[512]{0:T(512)S(1)} %get-tuple-element.172, s32[1024]{0:T(1024)S(1)} %pad_clamp_fusion.2), kind=kCustom, calls=%fused_computation.1 | custom fusion | bytes 6144 | tf_op jit(solution)/shard_map/gather | solution.py:62
  19.5 3.3 gather_fusion.2
  27.9 20.0 %all_to_all.54 = s32[128,1,8]{2,1,0:T(1,128)S(1)} all-to-all(s32[128,1,8]{2,1,0:T(1,128)S(1)} %bitcast.111), channel_id=1, replica_groups=mesh['rows'=32,'rep'=4] {'rows','rep'}, dimensions={0} | all-to-all | bytes 8192 | tf_op jit(solution)/shard_map/all_to_all | solution.py:82
  49.4 7.7 %gather_fusion.3 = bf16[1024,1024]{1,0:T(8,128)(2,1)S(1)} fusion(bf16[2048,1024]{1,0:T(8,128)(2,1)} %param.10, s32[1024]{0:T(1024)S(1)} %broadcast_clamp_fusion), kind=kCustom, calls=%fused_computation.3 | custom fusion | bytes 4198400 | tf_op jit(solution)/shard_map/jit(_take)/gather | solution.py:83
  58.7 4.9 %all-to-all-start.2 = ((bf16[128,8,1024]{2,1,0:T(8,128)(2,1)}), bf16[128,8,1024]{2,1,0:T(8,128)(2,1)S(1)}, u32[]{:S(2)}, u32[]{:S(2)}) async-start(bf16[128,8,1024]{2,1,0:T(8,128)(2,1)} %bitcast_select_fusion), calls=%async_computation.2 | async-start | bytes 4194304 | tf_op jit(solution)/shard_map/all_to_all | solution.py:85
  63.6 3.6 %slice_bitcast_fusion = (s32[1,512,4]{2,1,0:T(8,128)}, s32[1,512,4]{2,1,0:T(8,128)}, s32[1,512,4]{2,1,0:T(8,128)}, s32[1,512,4]{2,1,0:T(8,128)}, s32[1,512,4]{2,...) fusion(s32[512,128]{1,0:T(8,128)S(1)} %copy-done.1), kind=kLoop, calls=%fused_computation.30 | loop fusion | bytes 311296 | tf_op jit(solution)/shard_map/stack | solution.py:103
  116.3 6.7 %all-to-all-start = ((s32[32,512,4]{1,2,0:T(4,128)}), s32[32,512,4]{1,2,0:T(4,128)S(1)}, u32[]{:S(2)}, u32[]{:S(2)}) async-start(s32[32,512,4]{1,2,0:T(4,128)} %copy.88), calls=%async_computation | async-start | bytes 524288 | tf_op jit(solution)/shard_map/all_to_all | solution.py:102
  123.1 2.8 gather_fusion.4
  131.8 5.0 %all-to-all-start.3 = ((f32[512,32,32]{0,2,1:T(8,128)}), f32[512,32,32]{0,2,1:T(8,128)S(1)}, u32[]{:S(2)}, u32[]{:S(2)}) async-start(f32[512,32,32]{0,2,1:T(8,128)} %bitcast.108), calls=%async_computation.3 | async-start | bytes 4194304 | tf_op jit(solution)/shard_map/all_to_all | solution.py:100
  140.4 25.4 %all-to-all-done.3 = f32[512,32,32]{0,2,1:T(8,128)S(1)} async-done(((f32[512,32,32]{0,2,1:T(8,128)}), f32[512,32,32]{0,2,1:T(8,128)S(1)}, u32[]{:S(2)}, u32[]{:S(2)}) %all-to-all-start.3) | async-done | bytes 2097184 | tf_op jit(solution)/shard_map/all_to_all | solution.py:100
  165.8 4.6 %all-to-all-start.4 = ((s32[512,32,4]{0,2,1:T(4,128)}), s32[512,32,4]{0,2,1:T(4,128)}, u32[]{:S(2)}, u32[]{:S(2)}) async-start(s32[512,32,4]{0,2,1:T(4,128)} %all_to_all.45), calls=%async_computation.4 | async-start | bytes 524288 | tf_op jit(solution)/shard_map/all_to_all | solution.py:107
  173.0 4.0 %reshape.160 = f32[2,8192,4,8]{1,0,3,2:T(2,128)} reshape(f32[32,512,32]{1,0,2:T(8,128)} %copy.92) | data formatting | bytes 4194304 | tf_op jit(solution)/shard_map/reshape | solution.py:16
  179.3 111.4 %while.18 = (s32[]{:T(128)}, f32[4,256,8]{1,2,0:T(8,128)S(1)}, f32[4,256]{1,0:T(4,128)S(1)}, f32[4,256,8]{1,2,0:T(8,128)S(1)}, f32[4,256]{1,0:T(4,128)S(1)}, /*i...) while((s32[]{:T(128)}, f32[4,256,8]{1,2,0:T(8,128)S(1)}, ...), condition=%wide.region_8.9_spmd.clone.clone, body=%wide.region_5.8_spmd.clone.clone.sunk | while | flops 1677756416 | bytes 5406969 | solution.py:39
  186.1 10.9 %fusion.25 = f32[4,256,8]{1,2,0:T(8,128)S(1)} fusion(s32[8192,4]{0,1:T(4,128)S(1)} %constant_dynamic-slice_fusion.8, f32[1,8192,4,8]{1,0,3,2:T(1,128)S(1)} %constant_dynamic-slice_fusion.7, f32[4,256,8]{1,2,0:T(8,128)S(1)} %get-tuple-element.285, pred[]{:T(512)S(6)} %compare.12), kind=kOutput, calls=%fused_computation.18.clone.1 | convolution fusion | flops 813711360 | bytes 1245185 | tf_op jit(solution)/shard_map/while/body/eval_jaxpr/rsk,rsc->skc/dot_general | solution.py:27
  197.0 10.9 %fusion.22 = f32[4,256,8]{1,2,0:T(8,128)S(1)} fusion(s32[8192,4]{0,1:T(4,128)S(1)} %constant_dynamic-slice_fusion.6, f32[1,8192,4,8]{1,0,3,2:T(1,128)S(1)} %constant_dynamic-slice_fusion.7, f32[4,256,8]{1,2,0:T(8,128)S(1)} %get-tuple-element.283, pred[]{:T(512)S(6)} %compare.12), kind=kOutput, calls=%fused_computation.19.clone.1 | convolution fusion | flops 813711360 | bytes 1245185 | tf_op jit(solution)/shard_map/while/body/eval_jaxpr/rsk,rsc->skc/dot_general | solution.py:27
  207.9 13.5 %fusion.23 = f32[4,256]{1,0:T(4,128)S(1)} fusion(s32[8192,4]{0,1:T(4,128)S(1)} %constant_dynamic-slice_fusion.8), kind=kLoop, calls=%fused_computation.14.clone.1 | loop fusion | flops 25164800 | bytes 135168 | tf_op jit(solution)/shard_map/while/body/eval_jaxpr/reduce_sum | solution.py:34
  221.4 13.6 %fusion.24 = f32[4,256]{1,0:T(4,128)S(1)} fusion(s32[8192,4]{0,1:T(4,128)S(1)} %constant_dynamic-slice_fusion.6), kind=kLoop, calls=%fused_computation.15.clone.1 | loop fusion | flops 25164800 | bytes 135168 | tf_op jit(solution)/shard_map/while/body/eval_jaxpr/reduce_sum | solution.py:34
  241.8 10.9 %fusion.25 = f32[4,256,8]{1,2,0:T(8,128)S(1)} fusion(s32[8192,4]{0,1:T(4,128)S(1)} %constant_dynamic-slice_fusion.8, f32[1,8192,4,8]{1,0,3,2:T(1,128)S(1)} %constant_dynamic-slice_fusion.7, f32[4,256,8]{1,2,0:T(8,128)S(1)} %get-tuple-element.285, pred[]{:T(512)S(6)} %compare.12), kind=kOutput, calls=%fused_computation.18.clone.1 | convolution fusion | flops 813711360 | bytes 1245185 | tf_op jit(solution)/shard_map/while/body/eval_jaxpr/rsk,rsc->skc/dot_general | solution.py:27
  252.7 10.9 %fusion.22 = f32[4,256,8]{1,2,0:T(8,128)S(1)} fusion(s32[8192,4]{0,1:T(4,128)S(1)} %constant_dynamic-slice_fusion.6, f32[1,8192,4,8]{1,0,3,2:T(1,128)S(1)} %constant_dynamic-slice_fusion.7, f32[4,256,8]{1,2,0:T(8,128)S(1)} %get-tuple-element.283, pred[]{:T(512)S(6)} %compare.12), kind=kOutput, calls=%fused_computation.19.clone.1 | convolution fusion | flops 813711360 | bytes 1245185 | tf_op jit(solution)/shard_map/while/body/eval_jaxpr/rsk,rsc->skc/dot_general | solution.py:27
  263.6 13.5 %fusion.23 = f32[4,256]{1,0:T(4,128)S(1)} fusion(s32[8192,4]{0,1:T(4,128)S(1)} %constant_dynamic-slice_fusion.8), kind=kLoop, calls=%fused_computation.14.clone.1 | loop fusion | flops 25164800 | bytes 135168 | tf_op jit(solution)/shard_map/while/body/eval_jaxpr/reduce_sum | solution.py:34
  277.1 13.6 %fusion.24 = f32[4,256]{1,0:T(4,128)S(1)} fusion(s32[8192,4]{0,1:T(4,128)S(1)} %constant_dynamic-slice_fusion.6), kind=kLoop, calls=%fused_computation.15.clone.1 | loop fusion | flops 25164800 | bytes 135168 | tf_op jit(solution)/shard_map/while/body/eval_jaxpr/reduce_sum | solution.py:34
  291.4 40.0 %all-reduce.3.cloned.1.call-done = (f32[256,32]{0,1:T(8,128)}, f32[256,4]{0,1:T(4,128)}, f32[256,32]{0,1:T(8,128)}, f32[256,4]{0,1:T(4,128)}) async-done(((f32[256,32]{0,1:T(8,128)}, f32[256,4]{0,1:T(4,128)}, f32[256,32]{0,1:T(8,128)}, f32[256,4]{0,1:T(4,128)}), (f32[256,32]{0,1:T(8,128)}, f32[256,4]{0,1:T(4,128)}, f32[256,32]{0,1:T(8,128)}, f32[256,4]{0,1:T(4,128)})) %all-reduce.3.cloned.1.call-update) | async-done | bytes 73744 | tf_op jit(solution)/shard_map/psum | solution.py:48
  (110 shorter events, 85.2 us)
Async XLA Ops:
  7.2 1.2 copy-start
  7.2 4.4 %copy-start.9 = (s32[512]{0:T(512)S(1)}, s32[512]{0:T(512)}, u32[]{:S(2)}) copy-start(s32[512]{0:T(512)} %param.9) | copy-start | bytes 6148
  25.3 2.6 copy-start.7
  25.3 2.6 copy-start.8
  58.7 4.9 %copy-start.1 = (s32[512,128]{1,0:T(8,128)S(1)}, s32[512,128]{1,0:T(8,128)}, u32[]{:S(2)}) copy-start(s32[512,128]{1,0:T(8,128)} %param.12) | copy-start | bytes 786436
  58.7 57.7 %all-to-all-start.2 = ((bf16[128,8,1024]{2,1,0:T(8,128)(2,1)}), bf16[128,8,1024]{2,1,0:T(8,128)(2,1)S(1)}, u32[]{:S(2)}, u32[]{:S(2)}) async-start(bf16[128,8,1024]{2,1,0:T(8,128)(2,1)} %bitcast_select_fusion), calls=%async_computation.2 | async-start | bytes 4194304 | tf_op jit(solution)/shard_map/all_to_all | solution.py:85
  90.7 19.9 %copy-start.2 = (s32[1,512,4]{2,1,0:T(8,128)S(1)}, s32[1,512,4]{2,1,0:T(8,128)}, u32[]{:S(2)}) copy-start(s32[1,512,4]{2,1,0:T(8,128)} %get-tuple-element.194) | copy-start | bytes 24580
  116.3 15.5 %all-to-all-start = ((s32[32,512,4]{1,2,0:T(4,128)}), s32[32,512,4]{1,2,0:T(4,128)S(1)}, u32[]{:S(2)}, u32[]{:S(2)}) async-start(s32[32,512,4]{1,2,0:T(4,128)} %copy.88), calls=%async_computation | async-start | bytes 524288 | tf_op jit(solution)/shard_map/all_to_all | solution.py:102
  131.8 34.0 %all-to-all-start.3 = ((f32[512,32,32]{0,2,1:T(8,128)}), f32[512,32,32]{0,2,1:T(8,128)S(1)}, u32[]{:S(2)}, u32[]{:S(2)}) async-start(f32[512,32,32]{0,2,1:T(8,128)} %bitcast.108), calls=%async_computation.3 | async-start | bytes 4194304 | tf_op jit(solution)/shard_map/all_to_all | solution.py:100
  165.8 13.5 %all-to-all-start.4 = ((s32[512,32,4]{0,2,1:T(4,128)}), s32[512,32,4]{0,2,1:T(4,128)}, u32[]{:S(2)}, u32[]{:S(2)}) async-start(s32[512,32,4]{0,2,1:T(4,128)} %all_to_all.45), calls=%async_computation.4 | async-start | bytes 524288 | tf_op jit(solution)/shard_map/all_to_all | solution.py:107
  170.4 161.0 %all-reduce.3.cloned.1.call-start = ((), (), s32[]{:S(2)}) async-start(), calls=%async_computation.5 | async-start | bytes 147456 | tf_op jit(solution)/shard_map/psum | solution.py:48
  290.7 0.6 copy-start.3
  290.8 0.6 copy-start.4
  290.8 0.6 copy-start.5
  290.8 0.6 copy-start.6
Sparse Core Ops, SparseCore 0:
  291.5 39.8 all-reduce.2
